TPU v7x, 1024 devices: a whole 4x4x32 slice. The times are simulated.
1024 devices in a mesh: row: 16 (over z_hi, y), col: 64 (over z_lo, x, core).
Axes of the slice: x: 4, y: 4, z: 32 (z_hi: 4, z_lo: 8; z = z_hi * 8 + z_lo), core: 2. Of those that a mesh axis runs over, the one named last changes fastest.
Arguments:
- a_blocks: float32 [1024, 128, 128], P(('row', 'col')), may hold values from -0.5 to 0.5
- a_cols: int32 [1024], P(('row', 'col')), may hold values from 0 to 31, as said below
- b_blocks: float32 [32, 64, 128, 128], P('row', 'col'), may hold values from -6 to 6
- b_rows: int32 [32, 64], P('row', 'col'), may hold values from 0 to 31, as said below
- c_rows: int32 [12288], P(('row', 'col')), may hold values from 0 to 127, as said below
- c_cols: int32 [12288], P(('row', 'col')), may hold values from 0 to 255, as said below
Outputs:
- c_blocks: float32 [12288, 128, 128], P(('row', 'col'))
Inputs may be any that keep to these rules, and one draw needn't show every extreme that they name: `a_cols`: the 8 indices of one block row of A are distinct and form a run of consecutive indices modulo 32. `b_rows`: the 8 indices of one block column of B are distinct and form a run of consecutive indices modulo 32. The shard on the device with row index r holds block rows r * 8 to (r + 1) * 8 - 1; no pair (c_rows[t], c_cols[t]) repeats; every retained pair has at least one contracted index in common between its row of A and its column of B. `c_cols`: the shard on the device with col index c holds block columns c * 4 to (c + 1) * 4 - 1.
All inputs are finite; a program needn't handle non-finite values.
Results may differ from a plain program's by a relative error of at most 0.0003.
Values sent between devices are 32-bit elements; how exact they have to be, the bound alone decides.
A program may use at most 64 MiB of HBM per device.

v0:
```python
import jax
import jax.numpy as jnp
from jax import lax
from jax.sharding import PartitionSpec as P

KA = 8
KB = 8
RG = 8


def local(a_blocks, a_cols, b_blocks, b_rows, c_rows, c_cols):
    group_b, group_keys = (
        lax.all_gather(b_blocks, "row", axis=0, tiled=True),
        lax.all_gather(b_rows, "row", axis=0, tiled=True),
    )
    width = a_blocks.shape[1]
    cols_here = group_b.shape[0] // KB
    group_b = group_b.reshape(cols_here, KB, width, width)
    group_keys = group_keys.reshape(cols_here, KB)
    base_row = lax.axis_index("row") * RG
    base_col = lax.axis_index("col") * cols_here
    local_rows = c_rows - base_row
    local_cols = c_cols - base_col
    column_blocks = group_b[local_cols]
    column_keys = group_keys[local_cols]
    a_slots = local_rows[:, None] * KA + jnp.arange(KA, dtype=jnp.int32)[None, :]
    group_a, group_cols = (
        lax.all_gather(a_blocks, "col", axis=0, tiled=True),
        lax.all_gather(a_cols, "col", axis=0, tiled=True),
    )
    a_stack = group_a[a_slots]
    a_keys = group_cols[a_slots]
    matched = (a_keys[:, :, None] == column_keys[:, None, :]).astype(jnp.float32)
    b_stack = jnp.einsum("tsq,tqxy->tsxy", matched, column_blocks, precision=lax.Precision.HIGHEST)
    return jnp.einsum("tsxy,tsyz->txz", a_stack, b_stack, precision=lax.Precision.HIGHEST)


def solution(mesh):
    in_specs = (
        P(("row", "col"), None, None),
        P(("row", "col")),
        P("row", "col", None, None),
        P("row", "col"),
        P(("row", "col")),
        P(("row", "col")),
    )
    out_specs = P(("row", "col"), None, None)
    return jax.shard_map(local, mesh=mesh, in_specs=in_specs, out_specs=out_specs, check_vma=False)
```

profile of v0, /device:TPU:1, one launch (start us, length us, event | category | flops | bytes accessed | tf_op | source)
XLA Modules:
  0.0 341.3 jit_solution(8413525860699594587)
XLA Ops:
  6.5 0.0 copy-start
  6.5 0.0 copy-start.1
  6.5 0.0 all-gather.5.cloned.1.call-start
  6.5 0.7 all-gather.5.cloned.1.call-update
  7.3 0.0 all-gather.3.cloned.1.call-start
  7.3 0.7 all-gather.3.cloned.1.call-update
  8.0 0.7 subtract_multiply_fusion
  8.7 0.1 compare_select_fusion
  8.8 0.1 reshape.53
  9.5 1.3 dynamic-slice
  10.8 0.8 dynamic-update-slice
  11.5 23.1 %all-reduce = s32[64]{0:T(128)S(1)} all-reduce(s32[64]{0:T(128)S(1)} %dynamic-update-slice), channel_id=1, replica_groups=mesh['row'=16,'col'=64] {'col'}, use_global_device_ids=true, to_apply=%add | all-reduce | flops 64 | bytes 512
  34.6 1.2 gather_fusion.1
  35.9 0.1 reshape.60
  35.9 1.3 dynamic-slice.1
  37.9 0.0 copy-done
  37.9 0.1 bitcast_dynamic-update-slice_fusion
  38.0 34.2 %all-reduce.1 = s32[32]{0:T(128)S(1)} all-reduce(s32[32]{0:T(128)S(1)} %bitcast_dynamic-update-slice_fusion), channel_id=1, replica_groups=mesh['row'=16,'col'=64] {'row'}, use_global_device_ids=true, to_apply=%add.1 | all-reduce | flops 32 | bytes 256
  72.2 0.1 reshape.49
  72.3 0.0 copy-done.1
  72.3 0.6 gather_fusion.2
  72.9 119.7 %all-gather.5.cloned.1.call-done = f32[32,1,128,128]{3,2,1,0:T(8,128)} async-done(((f32[2,1,128,128]{3,2,1,0:T(8,128)}), f32[32,1,128,128]{3,2,1,0:T(8,128)}) %all-gather.5.cloned.1.call-update) | async-done | bytes 2097168 | tf_op jit(solution)/shard_map/all_gather | solution.py:13
  192.6 5.2 %gather_fusion.3 = f32[12,8,128,128]{3,2,1,0:T(8,128)} fusion(f32[4,8,128,128]{3,2,1,0:T(8,128)} %bitcast.18, s32[1024]{0:T(1024)S(1)} %pad_clamp_fusion), kind=kCustom, calls=%fused_computation.3 | custom fusion | bytes 12582960 | tf_op jit(solution)/shard_map/gather | solution.py:24
  197.8 11.7 %fusion.2 = f32[12,8,128,128]{3,1,2,0:T(8,128)} fusion(f32[12,8,128,128]{3,2,1,0:T(8,128)} %gather_fusion.3, s32[12,8]{1,0:T(8,128)S(1)} %gather_fusion.2, s32[12,8]{1,0:T(8,128)S(1)} %reshape.60), kind=kOutput, calls=%fused_computation.6 | convolution fusion | flops 150995712 | bytes 12583680 | tf_op jit(solution)/shard_map/tsq,tqxy->tsxy/dot_general | solution.py:34
  209.5 106.8 %all-gather.3.cloned.1.call-done = f32[64,128,128]{2,1,0:T(8,128)} async-done(((f32[1,128,128]{2,1,0:T(8,128)}), f32[64,128,128]{2,1,0:T(8,128)}) %all-gather.3.cloned.1.call-update) | async-done | bytes 4194320 | tf_op jit(solution)/shard_map/all_gather | solution.py:28
  316.3 5.8 %gather_fusion = f32[96,128,128]{2,1,0:T(8,128)} fusion(f32[64,128,128]{2,1,0:T(8,128)} %all-gather.3.cloned.1.call-done, s32[1024]{0:T(1024)S(1)} %pad_clamp_fusion.1), kind=kCustom, calls=%fused_computation | custom fusion | bytes 12583296 | tf_op jit(solution)/shard_map/gather | solution.py:31
  322.1 12.4 %fusion.4 = f32[12,128,128]{2,1,0:T(8,128)} fusion(f32[12,8,128,128]{3,2,1,0:T(8,128)} %bitcast.17, f32[12,8,128,128]{3,1,2,0:T(8,128)} %fusion.2), kind=kOutput, calls=%fused_computation.8 | convolution fusion | flops 2415919104 | bytes 13369344 | tf_op jit(solution)/shard_map/tsxy,tsyz->txz/dot_general | solution.py:35
  (5 shorter events, 0.0 us)
Async XLA Ops:
  6.5 31.4 %copy-start = (s32[2,1]{0,1:T(1,128)S(1)}, s32[2,1]{0,1:T(1,128)}, u32[]{:S(2)}) copy-start(s32[2,1]{0,1:T(1,128)} %param.9) | copy-start | bytes 28
  6.5 65.8 %copy-start.1 = (s32[12]{0:T(128)S(1)}, s32[12]{0:T(128)}, u32[]{:S(2)}) copy-start(s32[12]{0:T(128)} %param.11) | copy-start | bytes 148
  6.5 186.1 %all-gather.5.cloned.1.call-start = ((), (), s32[]{:S(2)}) async-start(), calls=%async_computation.1 | async-start | bytes 2228224 | tf_op jit(solution)/shard_map/all_gather | solution.py:13
  7.3 309.1 %all-gather.3.cloned.1.call-start = ((), (), s32[]{:S(2)}) async-start(), calls=%async_computation | async-start | bytes 4259840 | tf_op jit(solution)/shard_map/all_gather | solution.py:28
Sparse Core Ops, SparseCore 0:
  11.5 181.0 all-gather.4
  195.3 120.9 all-gather.2
where the time goes:
time: 342 us; the launch traced here: 341 us
  waiting for transfers between devices  228 us (67%)
  blocking collectives  57.3 us (17%)
  matrix products  24 us (7%)
  local copies, waits for them, and re-layouts  16.4 us (5%)
  between operations  14.8 us (4%)
    all_gather x1, waiting for transfers between devices, local(): lax.all_gather(b_blocks, 'row', axis=0, tiled=True)  120 us
    all_gather x1, waiting for transfers between devices, local(): lax.all_gather(a_blocks, 'col', axis=0, tiled=True)  107 us
    unnamed x2, blocking collectives  57.3 us
    dot_general x1, matrix products, local(): jnp.einsum('tsxy,tsyz->txz', a_stack, b_stack, precision=lax.Precision.HI...  12.4 us
    dot_general x1, matrix products, local(): jnp.einsum('tsq,tqxy->tsxy', matched, column_blocks, precision=lax.Precis...  11.7 us
  transfers between devices with their start and end apart: 2, of which 2 were waited for; matrix products, arithmetic and copies ran while one was open for 7% of the time, Pallas kernels for 0%

commit v1 on v0

v1 whole, which is shorter than its diff:
```python
import functools

import jax
import jax.numpy as jnp
from jax import lax
from jax.experimental import pallas as pl
from jax.experimental.pallas import tpu as pltpu
from jax.sharding import PartitionSpec as P

MESH = pl.DeviceIdType.MESH
BS = 128
KSPAN = 32
SLOTS = 8
NZH, NY, NZL, NX = 4, 4, 8, 4
CUTS = 2
ORDER = (
    "a0", "b0", "y", "k1", "a1", "b1", "k2", "a2", "b2", "x0", "k3", "a3",
    "b3", "x1", "k4", "c1", "a4", "b4", "c2", "x2", "s0", "a5", "b5", "c3",
    "x3", "s1", "a6", "c4", "x4", "s2", "p0", "n0.0.2", "a7", "c5", "x5", "s3",
    "x6", "s4", "c6", "p1", "p3", "n1.0.4", "n3.0.4", "n0.3.4", "x7", "s5", "s6", "s7",
    "n0.5.7", "n1.5.7", "n3.5.7", "t2", "p2", "w2",
)


def kernel(
    a_cols,
    b_rows,
    c_rows,
    c_cols,
    a_ref,
    b_ref,
    out_ref,
    abuf,
    bbuf,
    ah,
    al,
    lhs_h,
    lhs_l,
    rhs,
    cd,
    akv,
    bkv,
    aks,
    bks,
    first,
    where_is,
    a_recv,
    b_recv,
    az_send,
    ax_send,
    ac_send,
    bz_send,
    by_send,
    k_send,
    k_recv,
    loc,
):
    row, col = lax.axis_index("row"), lax.axis_index("col")
    zh, y = row // NY, row % NY
    zl, x, core = col // (2 * NX), (col // 2) % NX, col % 2

    def at_z(d):
        return (row, ((zl + d) % NZL) * 8 + x * 2 + core)

    def at_x(d):
        return (row, zl * 8 + ((x + d) % NX) * 2 + core)

    def at_core():
        return (row, zl * 8 + x * 2 + 1 - core)

    def at_zh(d):
        return (((zh + d) % NZH) * NY + y, col)

    def at_y(d):
        return (zh * NY + (y + d) % NY, col)

    barrier = pltpu.get_barrier_semaphore()
    partners = [at_z(d) for d in range(1, NZL)] + [at_x(d) for d in range(1, NX)]
    partners += [at_core()] + [at_zh(d) for d in range(1, NZH)] + [at_y(d) for d in range(1, NY)]
    for device in partners:
        pl.semaphore_signal(barrier, inc=1, device_id=device, device_id_type=MESH)
    own = [
        pltpu.make_async_copy(a_ref.at[0], abuf.at[col], loc.at[0]),
        pltpu.make_async_copy(b_ref.at[0, 0], bbuf.at[2 * row], loc.at[1]),
        pltpu.make_async_copy(b_ref.at[1, 0], bbuf.at[2 * row + 1], loc.at[2]),
    ]
    for c in own:
        c.start()
    akv[core * 32 + x * 8 + zl] = jnp.full((1, BS), a_cols[0], jnp.int32)
    lane = lax.broadcasted_iota(jnp.int32, (1, BS), 1)
    bkv[y * 4 + zh] = jnp.where(lane == 0, b_rows[0, 0], b_rows[1, 0])
    ah[64] = jnp.zeros((BS, BS), jnp.bfloat16)
    al[64] = jnp.zeros((BS, BS), jnp.bfloat16)
    with jax.named_scope("entry"):
        for c in own:
            c.wait()
        pl.semaphore_wait(barrier, len(partners))

    ends = []

    def copy(ref, send, recv, device):
        return pltpu.make_async_remote_copy(
            src_ref=ref, dst_ref=ref, send_sem=send, recv_sem=recv, device_id=device, device_id_type=MESH
        )

    def when(cond, f):
        if cond is None:
            f()
        else:
            pl.when(cond)(f)

    def go(make, cond=None):
        when(cond, lambda: make().start())
        ends.append(lambda: when(cond, lambda: make().wait_send()))

    def landed(ref, sem):
        pltpu.make_async_copy(ref, ref, sem).wait()

    def a_landed(slot):
        landed(abuf.at[slot], a_recv.at[slot])

    def a_z(slot, j, d, cond):
        go(lambda: copy(abuf.at[slot], az_send.at[j], a_recv.at[slot], at_z(d)), cond)

    def a_x(slot, j, cond):
        for n, d in enumerate((1, 3, 2)):
            go(lambda n=n, d=d: copy(abuf.at[slot], ax_send.at[3 * j + n], a_recv.at[slot], at_x(d)), cond)

    def a_core(slot, j, cond):
        go(lambda: copy(abuf.at[slot], ac_send.at[j], a_recv.at[slot], at_core()), cond)

    def line(k, sign):
        z = zl + sign * k
        return jnp.clip(z, 0, NZL - 1), (None if k == 0 else (z >= 0) & (z < NZL))

    def sides(k):
        return (0,) if k == 0 else (-1, 1)

    def number(k, sign):
        return 0 if k == 0 else 2 * k - 1 + (sign > 0)

    def a_line(k):
        for sign in sides(k):
            z, valid = line(k, sign)
            slot = z * 8 + x * 2 + core
            if k > 0:
                when(valid, lambda: a_landed(slot))
            more_right = (zl < NZL - 1) if valid is None else valid & (zl < NZL - 1)
            more_left = (zl > 0) if valid is None else valid & (zl > 0)
            if sign <= 0 and k < NZL - 1:
                a_z(slot, k, 1, more_right)
            if sign >= 0 and k < NZL - 1:
                a_z(slot, 8 + k, -1, more_left)
        for sign in sides(k):
            z, valid = line(k, sign)
            slot = z * 8 + x * 2 + core
            a_x(slot, number(k, sign), valid)
            a_core(slot, number(k, sign), valid)

    def a_from_x(k):
        for sign in sides(k):
            z, valid = line(k, sign)
            for n, d in enumerate((3, 1, 2)):
                slot = z * 8 + ((x + d) % NX) * 2 + core
                when(valid, lambda: a_landed(slot))
                a_core(slot, 16 + 3 * number(k, sign) + n, valid)

    def a_split(k):
        for sign in sides(k):
            z, valid = line(k, sign)

            def whole():
                for n in range(NX):
                    a_landed(z * 8 + n * 2 + 1 - core)

                def one(s, carry):
                    v = abuf[z * 8 + s]
                    hi = v.astype(jnp.bfloat16)
                    ah[z * 8 + s] = hi
                    al[z * 8 + s] = (v - hi.astype(jnp.float32)).astype(jnp.bfloat16)
                    return carry

                lax.fori_loop(0, SLOTS, one, 0)

            when(valid, whole)

    part = BS // CUTS

    def b_piece(q, i, h):
        return bbuf.at[2 * (((zh + q) % NZH) * NY + y) + i, pl.ds(h * part, part)]

    def b_sem(q, i, h):
        return b_recv.at[2 * (((zh + q) % NZH) * NY + y) + i, h]

    def b_z(q, i, h, d, j):
        return lambda: copy(b_piece(q, i, h), bz_send.at[j], b_sem(q, i, h), at_zh(d))

    state = {"come": 0, "y": 0}

    def b_y(q, i, h):
        for d in (1, 3, 2):
            j = state["y"]
            go(lambda j=j, d=d: copy(b_piece(q, i, h), by_send.at[j], b_sem(q, i, h), at_y(d)))
            state["y"] += 1

    to_right = [(0, i, h) for i in (0, 1) for h in range(CUTS)] + [(-1, 0, h) for h in range(CUTS)]
    to_left = [(0, i, h) for i in (1, 0) for h in range(CUTS)] + [(1, 1, h) for h in range(CUTS)]
    from_left = [(-1, i, h) for i in (0, 1) for h in range(CUTS)] + [(2, 0, h) for h in range(CUTS)]
    from_right = [(1, i, h) for i in (1, 0) for h in range(CUTS)] + [(2, 1, h) for h in range(CUTS)]

    def b_come(count):
        while state["come"] < count:
            for p in (from_left[state["come"]], from_right[state["come"]]):
                landed(b_piece(*p), b_sem(*p))
                b_y(*p)
            state["come"] += 1

    def b_send(k):
        go(b_z(*to_right[k], 1, 2 * k))
        go(b_z(*to_left[k], 3, 2 * k + 1))

    def b_own_y():
        for i in (0, 1):
            for h in range(CUTS):
                b_y(0, i, h)

    sems = {"n": 0}

    def key_go(ref, back, device):
        j = sems["n"]
        sems["n"] += 1
        go(lambda: copy(ref, k_send.at[j], k_recv.at[j], device))
        return lambda: landed(back, k_recv.at[j])

    def keys_1():
        out = []
        for d in range(1, NZL):
            base = core * 32 + x * 8
            out.append(key_go(akv.at[base + zl], akv.at[base + (zl - d) % NZL], at_z(d)))
        for d in range(1, NZH):
            out.append(key_go(bkv.at[y * 4 + zh], bkv.at[y * 4 + (zh - d) % NZH], at_zh(d)))
        return out

    def keys_2():
        out = []
        for d in range(1, NX):
            base = core * 32
            out.append(key_go(akv.at[pl.ds(base + x * 8, 8)], akv.at[pl.ds(base + ((x - d) % NX) * 8, 8)], at_x(d)))
        for d in range(1, NY):
            out.append(key_go(bkv.at[pl.ds(y * 4, 4)], bkv.at[pl.ds(((y - d) % NY) * 4, 4)], at_y(d)))
        return out

    def keys_3():
        return [key_go(akv.at[pl.ds(core * 32, 32)], akv.at[pl.ds((1 - core) * 32, 32)], at_core())]

    def keys_read():
        c0 = pltpu.make_async_copy(akv, aks, loc.at[3])
        c1 = pltpu.make_async_copy(bkv, bks, loc.at[4])
        c0.start()
        c1.start()
        c0.wait()
        c1.wait()

        def one(i, carry):
            keys = [aks[(s % 2) * 32 + (s // 2) * 8 + i, 0, 0] for s in range(SLOTS)]
            past = [lax.rem(k - keys[0] + KSPAN + KSPAN // 2, KSPAN) for k in keys]
            low = functools.reduce(jnp.minimum, past)
            first[i] = lax.rem(keys[0] + low + KSPAN - KSPAN // 2, KSPAN)
            for p in range(SLOTS):
                slot = sum(jnp.where(past[s] - low == p, s, 0) for s in range(SLOTS))
                where_is[i * 9 + p] = i * SLOTS + jnp.minimum(slot, SLOTS - 1)
            where_is[i * 9 + SLOTS] = 64
            return carry

        lax.fori_loop(0, 8, one, 0)

    def column_split(q):
        j = (zh + q) % NZH
        with jax.named_scope(f"column_wait{q}"):
            for d in range(1, NY):
                for i in (0, 1):
                    for h in range(CUTS):
                        slot = 2 * (j * NY + (y + d) % NY) + i
                        landed(bbuf.at[slot, pl.ds(h * part, part)], b_recv.at[slot, h])

        def one(s, carry):
            v = bbuf[j * SLOTS + s]
            hi = v.astype(jnp.bfloat16)
            rows = pl.ds(pl.multiple_of(s * BS, BS), BS)
            rhs[q, rows, :BS] = hi
            rhs[q, rows, BS:] = (v - hi.astype(jnp.float32)).astype(jnp.bfloat16)
            return carry

        lax.fori_loop(0, SLOTS, one, 0)

    def strip(q, i):
        j = (zh + q) % NZH
        rows = pl.ds(pl.multiple_of(i * BS, BS), BS)
        for s in range(SLOTS):
            key = bks[(s // 2) * 4 + j, 0, s % 2]
            at = where_is[i * 9 + jnp.minimum(lax.rem(key - first[i] + KSPAN, KSPAN), SLOTS)]
            lhs_h[rows, s * BS : (s + 1) * BS] = ah[at]
            lhs_l[rows, s * BS : (s + 1) * BS] = al[at]

    def multiply(q, i, count):
        j = (zh + q) % NZH
        rows = pl.ds(pl.multiple_of(i * BS, BS), count * BS)
        wide = jnp.dot(lhs_h[rows, :], rhs[q], preferred_element_type=jnp.float32)
        low = jnp.dot(lhs_l[rows, :], rhs[q, :, :BS], preferred_element_type=jnp.float32)
        total = wide[:, :BS] + wide[:, BS:] + low
        for n in range(count):
            cd[j * 8 + i + n] = total[n * BS : (n + 1) * BS]

    def strips(q):
        def one(i, carry):
            strip(q, i)
            return carry

        with jax.named_scope(f"strips{q}"):
            lax.fori_loop(0, 8, one, 0)

    def whole(q):
        def one(m, carry):
            multiply(q, 2 * m, 2)
            return carry

        with jax.named_scope(f"multiply{q}"):
            lax.fori_loop(0, 4, one, 0)

    def near(q, low, high):
        def one(i, carry):
            away = jnp.abs(i - zl)

            @pl.when((away >= low) & (away <= high))
            def _():
                strip(q, i)
                multiply(q, i, 1)

            return carry

        lax.fori_loop(0, 8, one, 0)

    steps = {
        "a": a_line,
        "x": a_from_x,
        "s": a_split,
        "b": b_send,
        "c": b_come,
        "y": b_own_y,
        "p": column_split,
        "n": near,
        "t": strips,
        "w": whole,
    }
    keys = []
    for step in ORDER:
        if step[0] == "k":
            for f in keys:
                f()
            keys = {"1": keys_1, "2": keys_2, "3": keys_3, "4": keys_read}[step[1]]() or []
        else:
            steps[step[0]](*[int(v) for v in step[1:].split(".") if v])

    def result(t, carry):
        out_ref[t] = cd[lax.rem(c_cols[t], 4) * 8 + lax.rem(c_rows[t], 8)]
        return carry

    with jax.named_scope("result"):
        lax.fori_loop(0, out_ref.shape[0], result, 0)
        for f in ends:
            f()


def local(a_blocks, a_cols, b_blocks, b_rows, c_rows, c_cols):
    smem, vmem = pl.BlockSpec(memory_space=pltpu.SMEM), pl.BlockSpec(memory_space=pltpu.VMEM)
    dma = pltpu.SemaphoreType.DMA
    return pl.pallas_call(
        kernel,
        out_shape=jax.ShapeDtypeStruct((c_rows.shape[0], BS, BS), jnp.float32),
        in_specs=[smem] * 4 + [pl.BlockSpec(memory_space=pl.ANY)] * 2,
        out_specs=vmem,
        scratch_shapes=[
            pltpu.VMEM((64, BS, BS), jnp.float32),
            pltpu.VMEM((32, BS, BS), jnp.float32),
            pltpu.VMEM((65, BS, BS), jnp.bfloat16),
            pltpu.VMEM((65, BS, BS), jnp.bfloat16),
            pltpu.VMEM((8 * BS, 8 * BS), jnp.bfloat16),
            pltpu.VMEM((8 * BS, 8 * BS), jnp.bfloat16),
            pltpu.VMEM((4, 8 * BS, 2 * BS), jnp.bfloat16),
            pltpu.VMEM((32, BS, BS), jnp.float32),
            pltpu.VMEM((64, 1, BS), jnp.int32),
            pltpu.VMEM((16, 1, BS), jnp.int32),
            pltpu.SMEM((64, 1, BS), jnp.int32),
            pltpu.SMEM((16, 1, BS), jnp.int32),
            pltpu.SMEM((8,), jnp.int32),
            pltpu.SMEM((72,), jnp.int32),
            dma((64,)),
            dma((32, CUTS)),
            dma((16,)),
            dma((48,)),
            dma((64,)),
            dma((6 * CUTS,)),
            dma((24 * CUTS,)),
            dma((17,)),
            dma((17,)),
            dma((5,)),
        ],
        compiler_params=pltpu.CompilerParams(collective_id=0, has_side_effects=True, vmem_limit_bytes=62 << 20),
        name="gather_and_multiply",
    )(a_cols, b_rows, c_rows, c_cols, a_blocks, b_blocks)


def solution(mesh):
    in_specs = (
        P(("row", "col"), None, None),
        P(("row", "col")),
        P("row", "col", None, None),
        P("row", "col"),
        P(("row", "col")),
        P(("row", "col")),
    )
    out_specs = P(("row", "col"), None, None)
    return jax.shard_map(local, mesh=mesh, in_specs=in_specs, out_specs=out_specs, check_vma=False)
```

time: 342 us -> 99 us (0.29)
  waiting for transfers between devices: 228 us -> 0 us
  Pallas kernels: 0 us -> 94.9 us
  blocking collectives: 57.3 us -> 0 us
  matrix products: 24 us -> 0 us
  between operations: 14.8 us -> 0.68 us
  local copies, waits for them, and re-layouts: 16.4 us -> 2.72 us
    all_gather x2 -> x0, waiting for transfers between devices: 227 us -> none  [the longest x1 120 us: local(): lax.all_gather(b_blocks, 'row', axis=0, tiled=True)]
    pallas_call x0 -> x1, Pallas kernels: none -> 94.9 us  [local(): pl.pallas_call(kernel, out_shape=jax.ShapeDtypeStruct((c_rows.shape[0], B...]
    unnamed x2 -> x0, blocking collectives: 57.3 us -> none
    dot_general x2 -> x0, matrix products: 24 us -> none  [the longest x1 12.4 us: local(): jnp.einsum('tsxy,tsyz->txz', a_stack, b_stack, precision=lax.Precision.HI...]
    gather x5 -> x0, local copies, waits for them, and re-layouts: 12.9 us -> none  [the longest x1 5.79 us: local(): a_stack = group_a[a_slots]]
  transfers between devices with their start and end apart: 2 -> 0, of which waited for: 2 -> 0; matrix products, arithmetic and copies ran while one was open for 7% -> 0% of each run, Pallas kernels for 0% -> 0%
where the time goes in v1:
time: 99 us; the launch traced here: 98.3 us
  Pallas kernels  94.9 us (96%)
  local copies, waits for them, and re-layouts  2.72 us (3%)
    pallas_call x1, Pallas kernels, local(): pl.pallas_call(kernel, out_shape=jax.ShapeDtypeStruct((c_rows.shape[0], B...  94.9 us
    unnamed x4, local copies, waits for them, and re-layouts  2.72 us

profile of v1, /device:TPU:1, one launch (start us, length us, event | category | flops | bytes accessed | tf_op | source)
XLA Modules:
  0.0 98.3 jit_solution(11415716733337304469)
XLA Ops:
  0.0 0.0 copy-start
  0.7 0.0 copy-done
  0.7 0.6 copy.7.b_rows
  1.3 94.9 %gather_and_multiply.1 = f32[12,128,128]{2,1,0:T(8,128)} custom-call(s32[1]{0:T(128)S(6)} %copy.9.a_cols, s32[2,1]{1,0:T(2,128)} %copy.7.b_rows, s32[12]{0:T(128)} %c_rows.1, s32[12]{0:T(128)} %c_cols.1, f32[1,128,128]{2,1,0:T(8,128)} %a_ref.1, f32[2,1,128,128]{3,2,1,0:T(8,128)} %b_ref.1), custom_call_target="tpu_custom_call" | custom-call | tf_op jit(solution)/shard_map/gather_and_multiply/pallas_call | solution.py:377
  96.3 2.1 %copy.10 = f32[12,128,128]{2,1,0:T(8,128)} copy(f32[12,128,128]{2,1,0:T(8,128)} %gather_and_multiply.1) | data formatting | bytes 1572864
Async XLA Ops:
  0.0 0.7 copy-start

commit v2 on v1

--- a/solution.py
+++ b/solution.py
@@ -16,9 +16,8 @@
 ORDER = (
     "a0", "b0", "y", "k1", "a1", "b1", "k2", "a2", "b2", "x0", "k3", "a3",
     "b3", "x1", "k4", "c1", "a4", "b4", "c2", "x2", "s0", "a5", "b5", "c3",
-    "x3", "s1", "a6", "c4", "x4", "s2", "p0", "n0.0.2", "a7", "c5", "x5", "s3",
-    "x6", "s4", "c6", "p1", "p3", "n1.0.4", "n3.0.4", "n0.3.4", "x7", "s5", "s6", "s7",
-    "n0.5.7", "n1.5.7", "n3.5.7", "t2", "p2", "w2",
+    "x3", "s1", "a6", "c4", "x4", "s2", "p0", "a7", "c5", "x5", "s3", "x6",
+    "s4", "c6", "p1", "p3", "x7", "s5", "s6", "s7", "p2", "w",
 )
 
 
@@ -32,12 +31,8 @@
     out_ref,
     abuf,
     bbuf,
-    ah,
-    al,
-    lhs_h,
-    lhs_l,
-    rhs,
-    cd,
+    left,
+    right,
     akv,
     bkv,
     aks,
@@ -89,8 +84,7 @@
     akv[core * 32 + x * 8 + zl] = jnp.full((1, BS), a_cols[0], jnp.int32)
     lane = lax.broadcasted_iota(jnp.int32, (1, BS), 1)
     bkv[y * 4 + zh] = jnp.where(lane == 0, b_rows[0, 0], b_rows[1, 0])
-    ah[64] = jnp.zeros((BS, BS), jnp.bfloat16)
-    al[64] = jnp.zeros((BS, BS), jnp.bfloat16)
+    left[64] = jnp.zeros((2 * BS, BS), jnp.bfloat16)
     with jax.named_scope("entry"):
         for c in own:
             c.wait()
@@ -176,8 +170,8 @@
                 def one(s, carry):
                     v = abuf[z * 8 + s]
                     hi = v.astype(jnp.bfloat16)
-                    ah[z * 8 + s] = hi
-                    al[z * 8 + s] = (v - hi.astype(jnp.float32)).astype(jnp.bfloat16)
+                    left[z * 8 + s, :BS] = hi
+                    left[z * 8 + s, BS:] = (v - hi.astype(jnp.float32)).astype(jnp.bfloat16)
                     return carry
 
                 lax.fori_loop(0, SLOTS, one, 0)
@@ -287,58 +281,27 @@
             v = bbuf[j * SLOTS + s]
             hi = v.astype(jnp.bfloat16)
             rows = pl.ds(pl.multiple_of(s * BS, BS), BS)
-            rhs[q, rows, :BS] = hi
-            rhs[q, rows, BS:] = (v - hi.astype(jnp.float32)).astype(jnp.bfloat16)
+            right[j, rows, :BS] = hi
+            right[j, rows, BS:] = (v - hi.astype(jnp.float32)).astype(jnp.bfloat16)
             return carry
 
         lax.fori_loop(0, SLOTS, one, 0)
 
-    def strip(q, i):
-        j = (zh + q) % NZH
-        rows = pl.ds(pl.multiple_of(i * BS, BS), BS)
-        for s in range(SLOTS):
-            key = bks[(s // 2) * 4 + j, 0, s % 2]
-            at = where_is[i * 9 + jnp.minimum(lax.rem(key - first[i] + KSPAN, KSPAN), SLOTS)]
-            lhs_h[rows, s * BS : (s + 1) * BS] = ah[at]
-            lhs_l[rows, s * BS : (s + 1) * BS] = al[at]
-
-    def multiply(q, i, count):
-        j = (zh + q) % NZH
-        rows = pl.ds(pl.multiple_of(i * BS, BS), count * BS)
-        wide = jnp.dot(lhs_h[rows, :], rhs[q], preferred_element_type=jnp.float32)
-        low = jnp.dot(lhs_l[rows, :], rhs[q, :, :BS], preferred_element_type=jnp.float32)
-        total = wide[:, :BS] + wide[:, BS:] + low
-        for n in range(count):
-            cd[j * 8 + i + n] = total[n * BS : (n + 1) * BS]
-
-    def strips(q):
-        def one(i, carry):
-            strip(q, i)
+    def pairs():
+        def one(t, carry):
+            i, j = lax.rem(c_rows[t], 8), lax.rem(c_cols[t], 4)
+            at = []
+            for s in range(SLOTS):
+                key = bks[(s // 2) * 4 + j, 0, s % 2]
+                at.append(where_is[i * 9 + jnp.minimum(lax.rem(key - first[i] + KSPAN, KSPAN), SLOTS)])
+            total = jnp.zeros((2 * BS, 2 * BS), jnp.float32)
+            for s in range(0, SLOTS, 2):
+                both = jnp.concatenate([left[at[s]], left[at[s + 1]]], axis=1)
+                total += jnp.dot(both, right[j, s * BS : (s + 2) * BS], preferred_element_type=jnp.float32)
+            out_ref[t] = total[:BS, :BS] + total[:BS, BS:] + total[BS:, :BS] + total[BS:, BS:]
             return carry
 
-        with jax.named_scope(f"strips{q}"):
-            lax.fori_loop(0, 8, one, 0)
-
-    def whole(q):
-        def one(m, carry):
-            multiply(q, 2 * m, 2)
-            return carry
-
-        with jax.named_scope(f"multiply{q}"):
-            lax.fori_loop(0, 4, one, 0)
-
-    def near(q, low, high):
-        def one(i, carry):
-            away = jnp.abs(i - zl)
-
-            @pl.when((away >= low) & (away <= high))
-            def _():
-                strip(q, i)
-                multiply(q, i, 1)
-
-            return carry
-
-        lax.fori_loop(0, 8, one, 0)
+        lax.fori_loop(0, out_ref.shape[0], one, 0)
 
     steps = {
         "a": a_line,
@@ -348,9 +311,7 @@
         "c": b_come,
         "y": b_own_y,
         "p": column_split,
-        "n": near,
-        "t": strips,
-        "w": whole,
+        "w": pairs,
     }
     keys = []
     for step in ORDER:
@@ -361,14 +322,8 @@
         else:
             steps[step[0]](*[int(v) for v in step[1:].split(".") if v])
 
-    def result(t, carry):
-        out_ref[t] = cd[lax.rem(c_cols[t], 4) * 8 + lax.rem(c_rows[t], 8)]
-        return carry
-
-    with jax.named_scope("result"):
-        lax.fori_loop(0, out_ref.shape[0], result, 0)
-        for f in ends:
-            f()
+    for f in ends:
+        f()
 
 
 def local(a_blocks, a_cols, b_blocks, b_rows, c_rows, c_cols):
@@ -377,17 +332,13 @@
     return pl.pallas_call(
         kernel,
         out_shape=jax.ShapeDtypeStruct((c_rows.shape[0], BS, BS), jnp.float32),
-        in_specs=[smem] * 4 + [pl.BlockSpec(memory_space=pl.ANY)] * 2,
+        in_specs=[smem] * 4 + [pl.BlockSpec(memory_space=pltpu.HBM)] * 2,
         out_specs=vmem,
         scratch_shapes=[
             pltpu.VMEM((64, BS, BS), jnp.float32),
             pltpu.VMEM((32, BS, BS), jnp.float32),
-            pltpu.VMEM((65, BS, BS), jnp.bfloat16),
-            pltpu.VMEM((65, BS, BS), jnp.bfloat16),
-            pltpu.VMEM((8 * BS, 8 * BS), jnp.bfloat16),
-            pltpu.VMEM((8 * BS, 8 * BS), jnp.bfloat16),
+            pltpu.VMEM((65, 2 * BS, BS), jnp.bfloat16),
             pltpu.VMEM((4, 8 * BS, 2 * BS), jnp.bfloat16),
-            pltpu.VMEM((32, BS, BS), jnp.float32),
             pltpu.VMEM((64, 1, BS), jnp.int32),
             pltpu.VMEM((16, 1, BS), jnp.int32),
             pltpu.SMEM((64, 1, BS), jnp.int32),
@@ -405,7 +356,7 @@
             dma((17,)),
             dma((5,)),
         ],
-        compiler_params=pltpu.CompilerParams(collective_id=0, has_side_effects=True, vmem_limit_bytes=62 << 20),
+        compiler_params=pltpu.CompilerParams(collective_id=0, has_side_effects=True, vmem_limit_bytes=40 << 20),
         name="gather_and_multiply",
     )(a_cols, b_rows, c_rows, c_cols, a_blocks, b_blocks)
 

time: 99 us -> 95.2 us (0.962)
  Pallas kernels: 94.9 us -> 90.4 us
    pallas_call x1, Pallas kernels: 94.9 us -> 90.4 us  [local(): pl.pallas_call(kernel, out_shape=jax.ShapeDtypeStruct((c_rows.shape[0], B...]
    unnamed x4 -> x12, local copies, waits for them, and re-layouts: 2.72 us -> 3.28 us
where the time goes in v2:
time: 95.2 us; the launch traced here: 94.4 us
  Pallas kernels  90.4 us (95%)
  local copies, waits for them, and re-layouts  3.28 us (3%)
    pallas_call x1, Pallas kernels, local(): pl.pallas_call(kernel, out_shape=jax.ShapeDtypeStruct((c_rows.shape[0], B...  90.4 us
    unnamed x12, local copies, waits for them, and re-layouts  3.28 us

profile of v2, /device:TPU:1, one launch (start us, length us, event | category | flops | bytes accessed | tf_op | source)
XLA Modules:
  0.0 94.4 jit_solution(15321227353683824287)
XLA Ops:
  0.0 0.0 copy-start.4
  0.7 0.0 copy-done.4
  0.7 0.0 copy-start.2
  0.7 0.0 copy-start.3
  0.7 0.1 copy.7.b_rows
  0.8 0.5 copy-done.2
  1.3 0.0 copy-done.3
  1.4 0.0 copy-start
  1.4 0.9 copy-done
  2.3 0.0 copy-start.1
  2.3 0.8 copy-done.1
  3.1 90.4 %gather_and_multiply.1 = f32[12,128,128]{2,1,0:T(8,128)S(1)} custom-call(s32[1]{0:T(128)S(6)} %copy.9.a_cols, s32[2,1]{1,0:T(2,128)S(1)} %copy.7.b_rows, s32[12]{0:T(128)S(1)} %copy-done.2, s32[12]{0:T(128)S(1)} %copy-done.3, f32[1,128,128]{2,1,0:T(8,128)S(1)} %copy-done.1, f32[2,1,128,128]{3,2,1,0:T(8,128)S(1)} %copy-done), custom_call_target="tpu_custom_call" | custom-call | tf_op jit(solution)/shard_map/gather_and_multiply/pallas_call | solution.py:332
  93.5 0.9 copy.10
Async XLA Ops:
  0.0 0.7 copy-start.4
  0.7 0.7 copy-start.2
  0.7 0.7 copy-start.3
  1.4 0.9 copy-start
  2.3 0.8 copy-start.1

commit v3 on v2

--- a/solution.py
+++ b/solution.py
@@ -14,7 +14,7 @@
 NZH, NY, NZL, NX = 4, 4, 8, 4
 CUTS = 2
 ORDER = (
-    "a0", "b0", "y", "k1", "a1", "b1", "k2", "a2", "b2", "x0", "k3", "a3",
+    "a0", "b0", "k1", "a1", "b1", "k2", "a2", "b2", "x0", "k3", "a3", "y",
     "b3", "x1", "k4", "c1", "a4", "b4", "c2", "x2", "s0", "a5", "b5", "c3",
     "x3", "s1", "a6", "c4", "x4", "s2", "p0", "a7", "c5", "x5", "s3", "x6",
     "s4", "c6", "p1", "p3", "x7", "s5", "s6", "s7", "p2", "w",

time: 95.2 us -> 94.6 us (level)
  no operation moved by 1% of the time
where the time goes in v3:
time: 94.6 us; the launch traced here: 93.6 us
  Pallas kernels  89.7 us (95%)
  local copies, waits for them, and re-layouts  3.28 us (3%)
    pallas_call x1, Pallas kernels, local(): pl.pallas_call(kernel, out_shape=jax.ShapeDtypeStruct((c_rows.shape[0], B...  89.7 us
    unnamed x12, local copies, waits for them, and re-layouts  3.28 us

profile of v3, /device:TPU:1, one launch (start us, length us, event | category | flops | bytes accessed | tf_op | source)
XLA Modules:
  0.0 93.6 jit_solution(10026957830319560741)
XLA Ops:
  0.0 0.0 copy-start.4
  0.7 0.0 copy-done.4
  0.7 0.0 copy-start.2
  0.7 0.0 copy-start.3
  0.7 0.1 copy.7.b_rows
  0.8 0.5 copy-done.2
  1.3 0.0 copy-done.3
  1.4 0.0 copy-start
  1.4 0.9 copy-done
  2.3 0.0 copy-start.1
  2.3 0.8 copy-done.1
  3.1 89.7 %gather_and_multiply.1 = f32[12,128,128]{2,1,0:T(8,128)S(1)} custom-call(s32[1]{0:T(128)S(6)} %copy.9.a_cols, s32[2,1]{1,0:T(2,128)S(1)} %copy.7.b_rows, s32[12]{0:T(128)S(1)} %copy-done.2, s32[12]{0:T(128)S(1)} %copy-done.3, f32[1,128,128]{2,1,0:T(8,128)S(1)} %copy-done.1, f32[2,1,128,128]{3,2,1,0:T(8,128)S(1)} %copy-done), custom_call_target="tpu_custom_call" | custom-call | tf_op jit(solution)/shard_map/gather_and_multiply/pallas_call | solution.py:332
  92.8 0.9 copy.10
Async XLA Ops:
  0.0 0.7 copy-start.4
  0.7 0.7 copy-start.2
  0.7 0.7 copy-start.3
  1.4 0.9 copy-start
  2.3 0.8 copy-start.1
